TPU v7x, 128 devices: a whole 4x4x4 slice. The times are simulated.
128 devices in a mesh: pipe: 16 (over z, y_lo, core), tensor: 8 (over x, y_hi).
Axes of the slice: x: 4, y: 4 (y_hi: 2, y_lo: 2; y = y_hi * 2 + y_lo), z: 4, core: 2. Of those that a mesh axis runs over, the one named last changes fastest.
Arguments:
- tokens: bfloat16 [1024, 8192], P('tensor', 'pipe'), may hold values from -6 to 6
- gate_weight: bfloat16 [8192, 28672], P('pipe', 'tensor'), may hold values from -0.0625 to 0.0625
- up_weight: bfloat16 [8192, 28672], P('pipe', 'tensor'), may hold values from -0.0625 to 0.0625
- down_weight: bfloat16 [28672, 8192], P('tensor', 'pipe'), may hold values from -0.03125 to 0.03125
- out_grad: bfloat16 [1024, 8192], P('tensor', 'pipe'), may hold values from -6 to 6
Outputs:
- output: bfloat16 [1024, 8192], P('tensor', 'pipe')
- input_grad: bfloat16 [1024, 8192], P('tensor', 'pipe')
- gate_grad: bfloat16 [8192, 28672], P('pipe', 'tensor')
- up_grad: bfloat16 [8192, 28672], P('pipe', 'tensor')
- down_grad: bfloat16 [28672, 8192], P('tensor', 'pipe')
All inputs are finite; a program needn't handle non-finite values.
Results may differ from a plain program's by a relative error of at most 0.005.
Values may be sent and summed in bfloat16 or wider, within the bound.
A program may use at most 256 MiB of HBM per device.

v0:
```python
import jax
import jax.numpy as jnp
from jax import lax
from jax.sharding import PartitionSpec as P


def contract_rows(left, right):
    return lax.dot_general(
        left, right, (((0,), (0,)), ((), ())), preferred_element_type=jnp.float32
    )


def contract_cols(left, right):
    return lax.dot_general(
        left, right, (((1,), (1,)), ((), ())), preferred_element_type=jnp.float32
    )


def forward_act(gate_value, up_value):
    sigma_gate = jax.nn.sigmoid(gate_value)
    return (gate_value * sigma_gate * up_value).astype(jnp.bfloat16)


def backward_act(hidden_grad, gate_value, up_value):
    sigma_gate = jax.nn.sigmoid(gate_value)
    swish_gate = gate_value * sigma_gate
    gate_delta = (
        hidden_grad * up_value * sigma_gate * (1.0 + gate_value * (1.0 - sigma_gate))
    ).astype(jnp.bfloat16)
    up_delta = (hidden_grad * swish_gate).astype(jnp.bfloat16)
    return (gate_delta, up_delta)


def per_device(tokens, gate_weight, up_weight, down_weight, out_grad):
    hidden_width = gate_weight.shape[1]
    all_inputs = lax.all_gather(tokens, "tensor", axis=0, tiled=True)
    rows_block = all_inputs
    gate_up = lax.psum_scatter(
        jnp.concatenate(
            [
                jnp.dot(rows_block, gate_weight, preferred_element_type=jnp.float32),
                jnp.dot(rows_block, up_weight, preferred_element_type=jnp.float32),
            ],
            axis=1,
        ),
        "pipe",
        scatter_dimension=0,
        tiled=True,
    )
    gate_value = gate_up[:, :hidden_width]
    up_value = gate_up[:, hidden_width:]
    own_hidden = forward_act(gate_value, up_value)
    all_hidden = lax.all_gather(own_hidden, "pipe", axis=0, tiled=True)
    rows_block = all_hidden
    output = lax.psum_scatter(
        jnp.dot(rows_block, down_weight, preferred_element_type=jnp.float32),
        "tensor",
        scatter_dimension=0,
        tiled=True,
    ).astype(jnp.bfloat16)
    all_grads = lax.all_gather(out_grad, "tensor", axis=0, tiled=True)
    rows_block = all_grads
    hidden_grad = lax.psum_scatter(
        contract_cols(rows_block, down_weight), "pipe", scatter_dimension=0, tiled=True
    )
    gate_delta, up_delta = backward_act(hidden_grad, gate_value, up_value)
    all_gate_delta, all_up_delta = (
        lax.all_gather(gate_delta, "pipe", axis=0, tiled=True),
        lax.all_gather(up_delta, "pipe", axis=0, tiled=True),
    )
    input_grad = lax.psum_scatter(
        contract_cols(all_gate_delta, gate_weight) + contract_cols(all_up_delta, up_weight),
        "tensor",
        scatter_dimension=0,
        tiled=True,
    ).astype(jnp.bfloat16)
    gate_grad = contract_rows(all_inputs, all_gate_delta).astype(jnp.bfloat16)
    up_grad = contract_rows(all_inputs, all_up_delta).astype(jnp.bfloat16)
    down_grad = contract_rows(all_hidden, all_grads).astype(jnp.bfloat16)
    return (output, input_grad, gate_grad, up_grad, down_grad)


def solution(mesh):
    placed = (
        P("tensor", "pipe"),
        P("pipe", "tensor"),
        P("pipe", "tensor"),
        P("tensor", "pipe"),
        P("tensor", "pipe"),
    )
    return jax.shard_map(
        per_device,
        mesh=mesh,
        in_specs=placed,
        out_specs=(
            P("tensor", "pipe"),
            P("tensor", "pipe"),
            P("pipe", "tensor"),
            P("pipe", "tensor"),
            P("tensor", "pipe"),
        ),
        check_vma=False,
    )
```

profile of v0, /device:TPU:1, one launch (start us, length us, event | category | flops | bytes accessed | tf_op | source)
XLA Modules:
  0.0 897.7 jit_solution(1604436133023479914)
XLA Ops:
  7.2 0.0 all-gather.10.cloned.1.call-start
  7.2 0.7 all-gather.10.cloned.1.call-update
  7.9 0.0 all-gather.6.cloned.1.call-start
  7.9 0.7 all-gather.6.cloned.1.call-update
  8.7 0.0 reduce-scatter.9.cloned.1.call-start
  8.7 51.3 %all-gather.10.cloned.1.call-done = bf16[1024,512]{1,0:T(8,128)(2,1)} async-done(((bf16[128,512]{1,0:T(8,128)(2,1)}), bf16[1024,512]{1,0:T(8,128)(2,1)}) %all-gather.10.cloned.1.call-update) | async-done | bytes 1048592 | tf_op jit(solution)/shard_map/all_gather | solution.py:61
  60.0 11.6 %fusion.6 = f32[1024,3584]{1,0:T(8,128)} fusion(bf16[1024,512]{1,0:T(8,128)(2,1)} %all-gather.10.cloned.1.call-done, bf16[3584,512]{1,0:T(8,128)(2,1)} %param.8), kind=kOutput, calls=%fused_computation.15 | convolution fusion | flops 3758096384 | bytes 19398656 | tf_op jit(solution)/shard_map/dot_general | solution.py:14
  71.6 0.0 reduce-scatter.9.cloned.1.call-update
  71.6 0.0 reduce-scatter.5.cloned.1.call-start
  71.7 36.9 %all-gather.6.cloned.1.call-done = bf16[1024,512]{1,0:T(8,128)(2,1)} async-done(((bf16[128,512]{1,0:T(8,128)(2,1)}), bf16[1024,512]{1,0:T(8,128)(2,1)}) %all-gather.6.cloned.1.call-update) | async-done | bytes 1048592 | tf_op jit(solution)/shard_map/all_gather | solution.py:36
  108.5 0.0 copy-start
  108.5 0.0 copy-start.2
  108.5 6.5 fusion.3
  115.0 0.0 copy-done
  115.0 0.0 copy-done.2
  115.0 4.0 fusion.4
  119.0 12.2 %pad_maximum_fusion = f32[1024,7168]{1,0:T(8,128)} fusion(f32[1024,3584]{1,0:T(8,128)S(1)} %fusion.4, f32[1024,3584]{1,0:T(8,128)S(1)} %fusion.3), kind=kLoop, calls=%fused_computation | loop fusion | flops 7340032 | bytes 58720256 | tf_op jit(solution)/shard_map/concatenate | solution.py:39
  131.2 0.0 reduce-scatter.5.cloned.1.call-update
  131.2 0.0 all-gather.12.cloned.1.call-start
  131.3 139.0 %reduce-scatter.9.cloned.1.call-done = f32[64,3584]{1,0:T(8,128)} async-done(((f32[1024,3584]{1,0:T(8,128)}), f32[64,3584]{1,0:T(8,128)}) %reduce-scatter.9.cloned.1.call-update) | async-done | bytes 917520 | tf_op jit(solution)/shard_map/reduce_scatter | solution.py:63
  270.3 310.3 %reduce-scatter.5.cloned.1.call-done = f32[64,7168]{1,0:T(8,128)} async-done(((f32[1024,7168]{1,0:T(8,128)}), f32[64,7168]{1,0:T(8,128)}) %reduce-scatter.5.cloned.1.call-update) | async-done | bytes 1835024 | tf_op jit(solution)/shard_map/reduce_scatter | solution.py:38
  580.6 3.2 multiply_convert_fusion
  583.8 0.0 all-gather.12.cloned.1.call-update
  583.8 0.0 all-gather.14.cloned.1.call-start
  583.9 0.5 all-gather.14.cloned.1.call-update
  584.4 0.0 all-gather.8.cloned.1.call-start
  584.5 0.7 all-gather.8.cloned.1.call-update
  585.2 0.2 reduce-scatter.11.cloned.1.call-start
  585.4 46.7 %all-gather.12.cloned.1.call-done = bf16[1024,3584]{1,0:T(8,128)(2,1)} async-done(((bf16[64,3584]{1,0:T(8,128)(2,1)}), bf16[1024,3584]{1,0:T(8,128)(2,1)}) %all-gather.12.cloned.1.call-update) | async-done | bytes 7340048 | tf_op jit(solution)/shard_map/all_gather | solution.py:68
  632.1 7.4 fusion.7
  639.4 43.0 %all-gather.14.cloned.1.call-done = bf16[1024,3584]{1,0:T(8,128)(2,1)} async-done(((bf16[64,3584]{1,0:T(8,128)(2,1)}), bf16[1024,3584]{1,0:T(8,128)(2,1)}) %all-gather.14.cloned.1.call-update) | async-done | bytes 7340048 | tf_op jit(solution)/shard_map/all_gather | solution.py:69
  682.4 9.5 %convolution_add_fusion = f32[1024,512]{1,0:T(8,128)} fusion(f32[1024,512]{1,0:T(8,128)S(1)} %fusion.7, bf16[1024,3584]{1,0:T(8,128)(2,1)} %all-gather.14.cloned.1.call-done, bf16[512,3584]{1,0:T(8,128)(2,1)} %param.7), kind=kOutput, calls=%fused_computation.6 | convolution fusion | flops 3758620672 | bytes 15204352 | tf_op jit(solution)/shard_map/dot_general | solution.py:14
  691.9 0.0 reduce-scatter.11.cloned.1.call-update
  692.0 0.0 reduce-scatter.7.cloned.1.call-start
  692.0 40.9 %all-gather.8.cloned.1.call-done = bf16[1024,3584]{1,0:T(8,128)(2,1)} async-done(((bf16[64,3584]{1,0:T(8,128)(2,1)}), bf16[1024,3584]{1,0:T(8,128)(2,1)}) %all-gather.8.cloned.1.call-update) | async-done | bytes 7340048 | tf_op jit(solution)/shard_map/all_gather | solution.py:53
  733.0 9.4 %fusion.5 = f32[1024,512]{1,0:T(8,128)} fusion(bf16[1024,3584]{1,0:T(8,128)(2,1)} %all-gather.8.cloned.1.call-done, bf16[3584,512]{1,0:T(8,128)(2,1)} %param.8), kind=kOutput, calls=%fused_computation.14 | convolution fusion | flops 3758096384 | bytes 13107200 | tf_op jit(solution)/shard_map/dot_general | solution.py:56
  742.4 0.0 reduce-scatter.7.cloned.1.call-update
  742.4 8.6 fusion
  751.0 5.9 copy.10
  756.9 8.7 fusion.1
  765.6 0.0 copy-start.1
  765.6 6.0 copy.11
  771.7 0.0 copy-done.1
  771.7 8.6 convolution_convert_fusion
  780.3 30.8 %reduce-scatter.11.cloned.1.call-done = f32[128,512]{1,0:T(8,128)} async-done(((f32[1024,512]{1,0:T(8,128)}), f32[128,512]{1,0:T(8,128)}) %reduce-scatter.11.cloned.1.call-update) | async-done | bytes 262160 | tf_op jit(solution)/shard_map/reduce_scatter | solution.py:71
  811.1 1.6 convert_element_type.34
  812.7 76.8 %reduce-scatter.7.cloned.1.call-done = f32[128,512]{1,0:T(8,128)} async-done(((f32[1024,512]{1,0:T(8,128)}), f32[128,512]{1,0:T(8,128)}) %reduce-scatter.7.cloned.1.call-update) | async-done | bytes 262160 | tf_op jit(solution)/shard_map/reduce_scatter | solution.py:55
  889.5 1.6 convert_element_type.31
Async XLA Ops:
  7.2 52.8 %all-gather.10.cloned.1.call-start = ((), (), s32[]{:S(2)}) async-start(), calls=%async_computation.8 | async-start | bytes 1179648 | tf_op jit(solution)/shard_map/all_gather | solution.py:61
  7.9 100.6 %all-gather.6.cloned.1.call-start = ((), (), s32[]{:S(2)}) async-start(), calls=%async_computation.4 | async-start | bytes 1179648 | tf_op jit(solution)/shard_map/all_gather | solution.py:36
  8.7 261.7 %reduce-scatter.9.cloned.1.call-start = ((), (), s32[]{:S(2)}) async-start(), calls=%async_computation.9 | async-start | bytes 15597568 | tf_op jit(solution)/shard_map/reduce_scatter | solution.py:63
  71.6 509.0 %reduce-scatter.5.cloned.1.call-start = ((), (), s32[]{:S(2)}) async-start(), calls=%async_computation.5 | async-start | bytes 31195136 | tf_op jit(solution)/shard_map/reduce_scatter | solution.py:38
  108.5 6.5 copy-start
  108.5 6.5 copy-start.2
  131.2 500.8 %all-gather.12.cloned.1.call-start = ((), (), s32[]{:S(2)}) async-start(), calls=%async_computation.10 | async-start | bytes 7798784 | tf_op jit(solution)/shard_map/all_gather | solution.py:68
  583.8 98.6 %all-gather.14.cloned.1.call-start = ((), (), s32[]{:S(2)}) async-start(), calls=%async_computation.11 | async-start | bytes 7798784 | tf_op jit(solution)/shard_map/all_gather | solution.py:69
  584.4 148.5 %all-gather.8.cloned.1.call-start = ((), (), s32[]{:S(2)}) async-start(), calls=%async_computation.6 | async-start | bytes 7798784 | tf_op jit(solution)/shard_map/all_gather | solution.py:53
  585.2 225.9 %reduce-scatter.11.cloned.1.call-start = ((), (), s32[]{:S(2)}) async-start(), calls=%async_computation.12 | async-start | bytes 2359296 | tf_op jit(solution)/shard_map/reduce_scatter | solution.py:71
  692.0 197.5 %reduce-scatter.7.cloned.1.call-start = ((), (), s32[]{:S(2)}) async-start(), calls=%async_computation.7 | async-start | bytes 2359296 | tf_op jit(solution)/shard_map/reduce_scatter | solution.py:55
  765.6 6.0 copy-start.1
Sparse Core Ops, SparseCore 0:
  10.3 49.5 all-gather.9
  62.3 46.1 all-gather.5
  110.9 159.3 reduce-scatter.8
  272.6 307.9 reduce-scatter.4
  583.9 48.0 all-gather.11
  634.2 48.1 all-gather.13
  684.7 48.1 all-gather.7
  736.7 74.3 reduce-scatter.10
  815.3 74.1 reduce-scatter.6
where the time goes:
time: 899 us; the launch traced here: 898 us
  waiting for transfers between devices  778 us (87%)
  matrix products  74.2 us (8%)
  other arithmetic  18.7 us (2%)
  between operations  13.9 us (2%)
  local copies, waits for them, and re-layouts  12 us (1%)
    reduce_scatter x1, waiting for transfers between devices, per_device(): lax.psum_scatter(jnp.concatenate([jnp.dot(rows_block, gate_weight, prefer...  310 us
    reduce_scatter x1, waiting for transfers between devices, per_device(): lax.psum_scatter(contract_cols(rows_block, down_weight), 'pipe', scatter_...  139 us
    reduce_scatter x1, waiting for transfers between devices, per_device(): lax.psum_scatter(jnp.dot(rows_block, down_weight, preferred_element_type=...  76.8 us
    all_gather x1, waiting for transfers between devices, per_device(): all_grads = lax.all_gather(out_grad, 'tensor', axis=0, tiled=True)  51.3 us
    all_gather x1, waiting for transfers between devices, per_device(): lax.all_gather(gate_delta, 'pipe', axis=0, tiled=True)  46.7 us
    all_gather x1, waiting for transfers between devices, per_device(): lax.all_gather(up_delta, 'pipe', axis=0, tiled=True)  43 us
    all_gather x1, waiting for transfers between devices, per_device(): all_hidden = lax.all_gather(own_hidden, 'pipe', axis=0, tiled=True)  40.9 us
    all_gather x1, waiting for transfers between devices, per_device(): all_inputs = lax.all_gather(tokens, 'tensor', axis=0, tiled=True)  36.9 us
  transfers between devices with their start and end apart: 9, of which 9 were waited for; matrix products, arithmetic and copies ran while one was open for 11% of the time, Pallas kernels for 0%

commit v1 on v0

v1 whole, which is shorter than its diff:
```python
import functools

import jax
import jax.numpy as jnp
from jax import lax
from jax.experimental import pallas as pl
from jax.experimental.pallas import tpu as pltpu
from jax.sharding import PartitionSpec as P

MESH = pl.DeviceIdType.MESH
BF = jnp.bfloat16
F32 = jnp.float32
CW = 128
SLOTS = 6
LAG_SUM = 2
LAG_USE = 4


def dot_nn(a, b):
    return lax.dot_general(a, b, (((1,), (0,)), ((), ())), preferred_element_type=F32)


def dot_nt(a, b):
    return lax.dot_general(a, b, (((1,), (1,)), ((), ())), preferred_element_type=F32)


def dot_tn(a, b):
    return lax.dot_general(a, b, (((0,), (0,)), ((), ())), preferred_element_type=F32)


def drain(ref, sem):
    pltpu.make_async_copy(ref, ref, sem).wait()


def kernel(
    dims,
    tok, wg, wu, wd, og,
    out, ig, gg, ug, dg,
    w_gu, w_d, x_all, x_t, o_all, h_all, d_all, out_acc, in_acc, part, part_h,
    s_gu, r_gu, own_gu, s_hg, r_hg, own_hg, gu, st_d, st_gu, rx, ts, tr, to,
    ld_w, rv_w, sd_w, ld_d, rv_d, sd_d, ld_a, rv_a, sd_a, rf_a, sf_a,
    sd_gu, rv_gu, sd_hg, rv_hg, sd_h, rv_h, sd_dl, rv_dl,
    l_dg, s_dg, r_dg, l_gu, s_gg, r_gg, s_x, r_x, s_t, r_t, l_o,
):
    nq, nt, td, dd, tq, fh, nc = dims
    pipe, t = lax.axis_index("pipe"), lax.axis_index("tensor")
    q, c = pipe // 2, pipe % 2
    oc = 1 - c
    tokens = nt * td

    def group(d):
        return ((q ^ d) * 2 + c, t)

    def shard(d):
        return (pipe, t ^ d)

    other = (q * 2 + oc, t)

    def send(src, dst, s, r, dev):
        pltpu.make_async_remote_copy(
            src_ref=src, dst_ref=dst, send_sem=s, recv_sem=r, device_id=dev, device_id_type=MESH
        ).start()

    def at(i, n):
        return pl.ds(pl.multiple_of(i * n, n), n)

    mine, theirs = at(c, dd), at(oc, dd)

    barrier = pltpu.get_barrier_semaphore()
    for d in range(1, nq):
        pl.semaphore_signal(barrier, inc=1, device_id=group(d), device_id_type=MESH)
    for d in range(1, nt):
        pl.semaphore_signal(barrier, inc=1, device_id=shard(d), device_id_type=MESH)
    pl.semaphore_signal(barrier, inc=1, device_id=other, device_id_type=MESH)
    pl.semaphore_wait(barrier, nq + nt - 1)

    for k, (src, dst) in enumerate(((tok, x_all), (og, o_all))):
        block = dst.at[at(t, td), mine]
        pltpu.make_async_copy(src, block, ld_a.at[k]).start()
        for d in range(1, nt):
            send(src, block, sd_a.at[k], rv_a.at[k, d], shard(d))
        send(src, block, sd_a.at[k], rf_a.at[k, 0], other)

        if k == 0:
            @pl.loop(0, nc)
            def _(i):
                keep = pl.ds(pl.multiple_of(c * fh + i * CW, CW), CW)
                give = pl.ds(pl.multiple_of(oc * fh + i * CW, CW), CW)
                for j, w in enumerate((wg, wu)):
                    place = w_gu.at[i, mine, pl.ds(j * CW, CW)]
                    pltpu.make_async_copy(w.at[:, keep], place, ld_w.at[i]).start()
                    send(w.at[:, give], place, sd_w, rv_w.at[i], other)

            pltpu.make_async_copy(wd.at[at(c, fh), :], w_d.at[:, mine], ld_d).start()
            send(wd.at[at(oc, fh), :], w_d.at[:, mine], sd_d, rv_d, other)

    def forward_blocks(k, ref):
        for d in range(1, nt):
            block = ref.at[at(t ^ d, td), mine]
            drain(block, rv_a.at[k, d])
            send(block, block, sf_a.at[k], rf_a.at[k, d], other)

    def await_blocks(k, ref):
        drain(ref.at[at(t, td), mine], ld_a.at[k])
        for d in range(nt):
            drain(ref.at[at(t ^ d, td), theirs], rf_a.at[k, d])

    forward_blocks(0, x_all)
    await_blocks(0, x_all)

    half = tokens // 2
    rows = tokens // 4

    def fwd_partial(i):
        slot = lax.rem(i, SLOTS)

        @pl.when(i >= SLOTS)
        def _():
            drain(s_gu.at[slot, pl.ds(0, (nq - 1) * tq)], sd_gu.at[slot])

        drain(w_gu.at[i, mine], ld_w.at[i])
        drain(w_gu.at[i, theirs], rv_w.at[i])

        @pl.loop(0, 2)
        def _(m):
            value = dot_nn(x_all[at(m, half), :], w_gu[i])
            part[at(m, half), :] = value
            s_gu[slot, at(m, half), :] = value.astype(BF)

        own_gu[slot] = part[at(q, tq), :]
        for d in range(1, nq):
            send(s_gu.at[slot, at(q ^ d, tq)], r_gu.at[slot, d - 1], sd_gu.at[slot], rv_gu.at[slot], group(d))

    def fwd_sum(i):
        slot = lax.rem(i, SLOTS)
        drain(r_gu.at[slot], rv_gu.at[slot])
        total = own_gu[slot]
        for d in range(nq - 1):
            total = total + r_gu[slot, d].astype(F32)
        gu[i] = total
        gate, up = total[:, :CW], total[:, CW:]
        h_all[i, at(q, tq), :] = (gate * jax.nn.sigmoid(gate) * up).astype(BF)
        block = h_all.at[i, at(q, tq)]
        for d in range(1, nq):
            send(block, block, sd_h.at[i], rv_h.at[i], group(d))

    def fwd_use(i):
        drain(h_all.at[i, pl.ds(0, (nq - 1) * tq)], rv_h.at[i])
        drain(h_all.at[i, pl.ds(0, (nq - 1) * tq)], sd_h.at[i])

        @pl.loop(0, 4)
        def _(m):
            value = dot_nn(h_all[i, at(m, rows), :], w_d[at(i, CW), :])

            @pl.when(i == 0)
            def _():
                out_acc[at(m, rows), :] = value

            @pl.when(i > 0)
            def _():
                out_acc[at(m, rows), :] += value

        s = lax.rem(i, 2)
        place = pl.ds(pl.multiple_of(c * fh + i * CW, CW), CW)

        @pl.when(i >= 2)
        def _():
            drain(st_d.at[s, :, mine], l_dg.at[s])
            drain(st_d.at[s, :, theirs], s_dg.at[s])

        st_d[s] = dot_tn(h_all[i], o_all[...]).astype(BF)
        pltpu.make_async_copy(st_d.at[s, :, mine], dg.at[place, :], l_dg.at[s]).start()
        send(st_d.at[s, :, theirs], dg.at[place, :], s_dg.at[s], r_dg, other)

    def bwd_partial(i):
        slot = lax.rem(i, SLOTS)

        @pl.when(i >= SLOTS)
        def _():
            drain(s_hg.at[slot, pl.ds(0, (nq - 1) * tq)], sd_hg.at[slot])

        @pl.loop(0, 2)
        def _(m):
            value = dot_nt(o_all[at(m, half), :], w_d[at(i, CW), :])
            part_h[at(m, half), :] = value
            s_hg[slot, at(m, half), :] = value.astype(BF)

        own_hg[slot] = part_h[at(q, tq), :]
        for d in range(1, nq):
            send(s_hg.at[slot, at(q ^ d, tq)], r_hg.at[slot, d - 1], sd_hg.at[slot], rv_hg.at[slot], group(d))

    def bwd_sum(i):
        slot = lax.rem(i, SLOTS)
        drain(r_hg.at[slot], rv_hg.at[slot])
        total = own_hg[slot]
        for d in range(nq - 1):
            total = total + r_hg[slot, d].astype(F32)
        gate, up = gu[i, :, :CW], gu[i, :, CW:]
        sigma = jax.nn.sigmoid(gate)
        d_all[i, at(q, tq), :CW] = (total * up * sigma * (1.0 + gate * (1.0 - sigma))).astype(BF)
        d_all[i, at(q, tq), CW:] = (total * (gate * sigma)).astype(BF)
        block = d_all.at[i, at(q, tq)]
        for d in range(1, nq):
            send(block, block, sd_dl.at[i], rv_dl.at[i], group(d))

    def bwd_use(i):
        drain(d_all.at[i, pl.ds(0, (nq - 1) * tq)], rv_dl.at[i])
        drain(d_all.at[i, pl.ds(0, (nq - 1) * tq)], sd_dl.at[i])
        s = lax.rem(i, 2)
        place = pl.ds(pl.multiple_of(c * fh + i * CW, CW), CW)

        @pl.when(i >= 2)
        def _():
            drain(st_gu.at[s, mine], l_gu.at[s])
            drain(st_gu.at[s, theirs], s_gg.at[s])

        @pl.loop(0, 2)
        def _(m):
            st_gu[s, at(m, dd), :] = dot_nn(x_t[at(m, dd), :], d_all[i]).astype(BF)

        for j, (grad, r) in enumerate(((gg, 0), (ug, 1))):
            lanes = pl.ds(j * CW, CW)
            pltpu.make_async_copy(st_gu.at[s, mine, lanes], grad.at[:, place], l_gu.at[s]).start()
            send(st_gu.at[s, theirs, lanes], grad.at[:, place], s_gg.at[s], r_gg.at[r], other)

        @pl.loop(0, 4)
        def _(m):
            value = dot_nt(d_all[i, at(m, rows), :], w_gu[i])

            @pl.when(i == 0)
            def _():
                in_acc[at(m, rows), :] = value

            @pl.when(i > 0)
            def _():
                in_acc[at(m, rows), :] += value

    def reduce_pair(k, acc):
        send(acc.at[:, theirs], rx.at[k], s_x.at[k], r_x.at[k], other)

    def reduce_send(k, acc):
        drain(rx.at[k], r_x.at[k])

        @pl.loop(0, nt)
        def _(j):
            value = acc[at(j, td), mine] + rx[k, at(j, td), :]
            rx[k, at(j, td), :] = value
            ts[k, at(j, td), :] = value.astype(BF)

        for d in range(1, nt):
            send(ts.at[k, at(t ^ d, td)], tr.at[k, d - 1], s_t.at[k], r_t.at[k], shard(d))

    def reduce_done(k, result):
        drain(tr.at[k], r_t.at[k])
        total = rx[k, at(t, td), :]
        for d in range(nt - 1):
            total = total + tr[k, d].astype(F32)
        to[k] = total.astype(BF)
        pltpu.make_async_copy(to.at[k], result, l_o.at[k]).start()
        drain(rx.at[k], s_x.at[k])
        drain(ts.at[k, pl.ds(0, (nt - 1) * td)], s_t.at[k])

    steps = 2 * nc + LAG_USE

    @pl.loop(0, steps)
    def _(v):
        @pl.when(v < nc)
        def _():
            fwd_partial(v)

        @pl.when((v >= nc) & (v < 2 * nc))
        def _():
            bwd_partial(v - nc)

        @pl.when(v == LAG_USE - 1)
        def _():
            forward_blocks(1, o_all)
            drain(w_d.at[:, mine], ld_d)
            drain(w_d.at[:, theirs], rv_d)

            @pl.loop(0, nt)
            def _(j):
                x_t[:, at(j, td)] = x_all[at(j, td), :].T

        @pl.when((v >= LAG_SUM) & (v < nc + LAG_SUM))
        def _():
            fwd_sum(v - LAG_SUM)

        @pl.when((v >= nc + LAG_SUM) & (v < 2 * nc + LAG_SUM))
        def _():
            bwd_sum(v - nc - LAG_SUM)

        @pl.when(v == LAG_USE)
        def _():
            await_blocks(1, o_all)

        @pl.when((v >= LAG_USE) & (v < nc + LAG_USE))
        def _():
            fwd_use(v - LAG_USE)

        @pl.when(v >= nc + LAG_USE)
        def _():
            bwd_use(v - nc - LAG_USE)

        @pl.when(v == nc + LAG_USE)
        def _():
            reduce_pair(0, out_acc)

        @pl.when(v == nc + LAG_USE + 1)
        def _():
            reduce_send(0, out_acc)

        @pl.when(v == nc + LAG_USE + 5)
        def _():
            reduce_done(0, out)

    reduce_pair(1, in_acc)
    reduce_send(1, in_acc)
    reduce_done(1, ig)

    for s in range(SLOTS):
        drain(s_gu.at[s, pl.ds(0, (nq - 1) * tq)], sd_gu.at[s])
        drain(s_hg.at[s, pl.ds(0, (nq - 1) * tq)], sd_hg.at[s])
    for s in range(2):
        drain(st_d.at[s, :, mine], l_dg.at[s])
        drain(st_d.at[s, :, theirs], s_dg.at[s])
        drain(st_gu.at[s, mine], l_gu.at[s])
        drain(st_gu.at[s, theirs], s_gg.at[s])
        drain(to.at[s], l_o.at[s])
    partner = at(oc, fh)
    drain(dg.at[partner, :], r_dg)
    drain(gg.at[:, partner], r_gg.at[0])
    drain(ug.at[:, partner], r_gg.at[1])
    drain(w_gu.at[:, mine], sd_w)
    drain(w_d.at[:, mine], sd_d)
    for k, ref in enumerate((x_all, o_all)):
        drain(ref.at[:, pl.ds(0, dd)], sd_a.at[k])
        drain(ref.at[pl.ds(0, (nt - 1) * td), pl.ds(0, dd)], sf_a.at[k])


def per_device(tokens, gate_weight, up_weight, down_weight, out_grad):
    nq, nt = lax.axis_size("pipe") // 2, lax.axis_size("tensor")
    td, dd = tokens.shape
    ff = gate_weight.shape[1]
    fh = ff // 2
    nc = fh // CW
    n = nt * td
    tq = n // nq
    d2 = 2 * dd
    vmem = pltpu.VMEM
    dma = pltpu.SemaphoreType.DMA
    anywhere = pl.BlockSpec(memory_space=pl.ANY)
    return pl.pallas_call(
        functools.partial(kernel, (nq, nt, td, dd, tq, fh, nc)),
        name="swiglu",
        out_shape=(
            jax.ShapeDtypeStruct((td, dd), BF),
            jax.ShapeDtypeStruct((td, dd), BF),
            jax.ShapeDtypeStruct((dd, ff), BF),
            jax.ShapeDtypeStruct((dd, ff), BF),
            jax.ShapeDtypeStruct((ff, dd), BF),
        ),
        in_specs=[anywhere] * 5,
        out_specs=(anywhere,) * 5,
        scratch_shapes=[
            vmem((nc, d2, 2 * CW), BF),
            vmem((fh, d2), BF),
            vmem((n, d2), BF),
            vmem((d2, n), BF),
            vmem((n, d2), BF),
            vmem((nc, n, CW), BF),
            vmem((nc, n, 2 * CW), BF),
            vmem((n, d2), F32),
            vmem((n, d2), F32),
            vmem((n, 2 * CW), F32),
            vmem((n, CW), F32),
            vmem((SLOTS, n, 2 * CW), BF),
            vmem((SLOTS, nq - 1, tq, 2 * CW), BF),
            vmem((SLOTS, tq, 2 * CW), F32),
            vmem((SLOTS, n, CW), BF),
            vmem((SLOTS, nq - 1, tq, CW), BF),
            vmem((SLOTS, tq, CW), F32),
            vmem((nc, tq, 2 * CW), F32),
            vmem((2, CW, d2), BF),
            vmem((2, d2, 2 * CW), BF),
            vmem((2, n, dd), F32),
            vmem((2, n, dd), BF),
            vmem((2, nt - 1, td, dd), BF),
            vmem((2, td, dd), BF),
            dma((nc,)), dma((nc,)), dma,
            dma, dma, dma,
            dma((2,)), dma((2, nt)), dma((2,)), dma((2, nt)), dma((2,)),
            dma((SLOTS,)), dma((SLOTS,)), dma((SLOTS,)), dma((SLOTS,)),
            dma((nc,)), dma((nc,)), dma((nc,)), dma((nc,)),
            dma((2,)), dma((2,)), dma,
            dma((2,)), dma((2,)), dma((2,)),
            dma((2,)), dma((2,)), dma((2,)), dma((2,)), dma((2,)),
        ],
        compiler_params=pltpu.CompilerParams(
            collective_id=0, has_side_effects=True, vmem_limit_bytes=63 * 1024 * 1024
        ),
        cost_estimate=pl.CostEstimate(flops=18 * n * d2 * fh, bytes_accessed=6 * ff * dd * 2, transcendentals=0),
    )(tokens, gate_weight, up_weight, down_weight, out_grad)


def solution(mesh):
    act, wide, tall = P("tensor", "pipe"), P("pipe", "tensor"), P("tensor", "pipe")
    return jax.shard_map(
        per_device,
        mesh=mesh,
        in_specs=(act, wide, wide, tall, act),
        out_specs=(act, act, wide, wide, tall),
        check_vma=False,
    )
```

time: 899 us -> 331 us (0.37)
  waiting for transfers between devices: 778 us -> 0 us
  Pallas kernels: 0 us -> 315 us
  matrix products: 74.2 us -> 0 us
  other arithmetic: 18.7 us -> 0 us
  between operations: 13.9 us -> 0.64 us
    reduce_scatter x4 -> x0, waiting for transfers between devices: 557 us -> none  [the longest x1 310 us: per_device(): lax.psum_scatter(jnp.concatenate([jnp.dot(rows_block, gate_weight, prefer...]
    pallas_call x0 -> x1, Pallas kernels: none -> 315 us  [per_device(): pl.pallas_call(functools.partial(kernel, (nq, nt, td, dd, tq, fh, nc)), n...]
    all_gather x5 -> x0, waiting for transfers between devices: 219 us -> none  [the longest x1 51.3 us: per_device(): all_grads = lax.all_gather(out_grad, 'tensor', axis=0, tiled=True)]
    dot_general x9 -> x0, matrix products: 74.2 us -> none  [the longest x3 28.5 us: contract_cols(): lax.dot_general(left, right, (((1,), (1,)), ((), ())), preferred_element_...]
    concatenate x1 -> x0, other arithmetic: 12.2 us -> none  [per_device(): jnp.concatenate([jnp.dot(rows_block, gate_weight, preferred_element_type=...]
  transfers between devices with their start and end apart: 9 -> 0, of which waited for: 9 -> 0; matrix products, arithmetic and copies ran while one was open for 11% -> 0% of each run, Pallas kernels for 0% -> 0%
where the time goes in v1:
time: 331 us; the launch traced here: 328 us
  Pallas kernels  315 us (95%)
  local copies, waits for them, and re-layouts  12.6 us (4%)
    pallas_call x1, Pallas kernels, per_device(): pl.pallas_call(functools.partial(kernel, (nq, nt, td, dd, tq, fh, nc)), n...  315 us
    unnamed x9, local copies, waits for them, and re-layouts  12.6 us

profile of v1, /device:TPU:1, one launch (start us, length us, event | category | flops | bytes accessed | tf_op | source)
XLA Modules:
  0.0 327.8 jit_solution(11762940785024031100)
XLA Ops:
  0.6 314.5 %swiglu.1 = (bf16[128,512]{1,0:T(8,128)(2,1)}, bf16[128,512]{1,0:T(8,128)(2,1)}, bf16[512,3584]{1,0:T(8,128)(2,1)}, bf16[512,3584]{1,0:T(8,128)(2,1)}, bf16[3584,512]{1,0:T(8,128)(2,1)}) custom-call(bf16[128,512]{1,0:T(8,128)(2,1)} %tok.1, bf16[512,3584]{1,0:T(8,128)(2,1)} %wg.1, bf16[512,3584]{1,0:T(8,128)(2,1)} %wu.1, bf16[3584,512]{1,0:T(8,128)(2,1)} %wd.1, ...), custom_call_target="tpu_custom_call" | custom-call | flops 33822867456 | bytes 22020096 | tf_op jit(solution)/shard_map/swiglu/pallas_call | solution.py:353
  315.2 1.6 copy.15
  316.7 1.6 copy.16
  318.3 0.0 copy-start.1
  318.3 4.3 %copy.17 = bf16[512,3584]{1,0:T(8,128)(2,1)} copy(bf16[512,3584]{1,0:T(8,128)(2,1)} %get-tuple-element.12) | data formatting | bytes 7340032
  322.6 0.0 copy-done.1
  322.6 0.0 copy-start
  322.6 1.9 copy.18
  324.4 1.5 copy-done
  325.9 1.8 copy.19
Async XLA Ops:
  318.3 4.3 %copy-start.1 = (bf16[512,3584]{1,0:T(8,128)(2,1)S(1)}, bf16[512,3584]{1,0:T(8,128)(2,1)}, u32[]{:S(2)}) copy-start(bf16[512,3584]{1,0:T(8,128)(2,1)} %get-tuple-element.13) | copy-start | bytes 11010052
  322.6 3.4 %copy-start = (bf16[3584,512]{1,0:T(8,128)(2,1)S(1)}, bf16[3584,512]{1,0:T(8,128)(2,1)}, u32[]{:S(2)}) copy-start(bf16[3584,512]{1,0:T(8,128)(2,1)} %get-tuple-element.14) | copy-start | bytes 11010052

commit v2 on v1

v2 whole, which is shorter than its diff:
```python
import functools

import jax
import jax.numpy as jnp
from jax import lax
from jax.experimental import pallas as pl
from jax.experimental.pallas import tpu as pltpu
from jax.sharding import PartitionSpec as P

MESH = pl.DeviceIdType.MESH
BF = jnp.bfloat16
F32 = jnp.float32
NZ = 4
CW = 128
SLOTS = 8
LAG = (2, 4, 6, 8, 10, 12)


def dot_nn(a, b):
    return lax.dot_general(a, b, (((1,), (0,)), ((), ())), preferred_element_type=F32)


def dot_nt(a, b):
    return lax.dot_general(a, b, (((1,), (1,)), ((), ())), preferred_element_type=F32)


def dot_tn(a, b):
    return lax.dot_general(a, b, (((0,), (0,)), ((), ())), preferred_element_type=F32)


def drain(ref, sem):
    pltpu.make_async_copy(ref, ref, sem).wait()


def kernel(
    dims,
    tok, wg, wu, wd, og,
    out, ig, gg, ug, dg,
    w_gu, w_d, x_all, x_t, o_all, h_all, d_all, out_acc, in_acc, part,
    keep, s1, s2, s3, r1, r2, r3, gu, st_d, st_gu, rx, ry, ta, ra, tb, rb, tc, rc, to,
    ld_w, rv_w, sd_w, ld_d, rv_d, sd_d, ld_a, rv_a, sd_a, rf_a, sf_a,
    sd_1, sd_2, sd_3, rv_1, rv_2, rv_3, rv_4, sd_h, rv_h, sd_dl, rv_dl,
    l_dg, s_dg, r_dg, l_gu, s_gg, r_gg, s_x, r_x, s_a, r_a, s_b, r_b, s_c, r_c, s_y, r_y, l_o,
):
    nt, td, dd, tq, fh, nc = dims
    pipe, t = lax.axis_index("pipe"), lax.axis_index("tensor")
    q, c = pipe // 2, pipe % 2
    oc = 1 - c
    tokens = nt * td

    z, y = q // 2, q % 2

    def chip(dz, dy):
        return lax.rem(z + dz + NZ, NZ) * 2 + (y ^ dy)

    up_z, down_z, over_y = ((chip(dz, dy) * 2 + c, t) for dz, dy in ((1, 0), (-1, 0), (0, 1)))

    def shard(d):
        return (pipe, t ^ d)

    other = (q * 2 + oc, t)

    def send(src, dst, s, r, dev):
        pltpu.make_async_remote_copy(
            src_ref=src, dst_ref=dst, send_sem=s, recv_sem=r, device_id=dev, device_id_type=MESH
        ).start()

    def at(i, n):
        return pl.ds(pl.multiple_of(i * n, n), n)

    mine, theirs = at(c, dd), at(oc, dd)

    barrier = pltpu.get_barrier_semaphore()
    for near in (up_z, down_z, over_y):
        pl.semaphore_signal(barrier, inc=1, device_id=near, device_id_type=MESH)
    for d in (1, 2, 4, 6):
        pl.semaphore_signal(barrier, inc=1, device_id=shard(d), device_id_type=MESH)
    pl.semaphore_signal(barrier, inc=1, device_id=other, device_id_type=MESH)
    pl.semaphore_wait(barrier, 8)

    def spread(k, src, dst):
        block = dst.at[at(t, td), mine]
        pltpu.make_async_copy(src, block, ld_a.at[k]).start()
        for d in (1, 2, 4, 6):
            send(src, block, sd_a.at[k], rv_a.at[k, d], shard(d))
        send(src, block, sd_a.at[k], rf_a.at[k, 0], other)

    spread(0, tok, x_all)

    @pl.loop(0, nc)
    def _(i):
        keep_cols = pl.ds(pl.multiple_of(c * fh + i * CW, CW), CW)
        give_cols = pl.ds(pl.multiple_of(oc * fh + i * CW, CW), CW)
        for j, w in enumerate((wg, wu)):
            place = w_gu.at[i, mine, pl.ds(j * CW, CW)]
            pltpu.make_async_copy(w.at[:, keep_cols], place, ld_w.at[i]).start()
            send(w.at[:, give_cols], place, sd_w, rv_w.at[i], other)

    pltpu.make_async_copy(wd.at[at(c, fh), :], w_d.at[:, mine], ld_d).start()
    send(wd.at[at(oc, fh), :], w_d.at[:, mine], sd_d, rv_d, other)

    hd = dd // 2

    def forward_blocks(k, ref):
        left = pl.ds(pl.multiple_of(c * dd, hd), hd)
        right = pl.ds(pl.multiple_of(c * dd + hd, hd), hd)
        for d in (1, 2, 4, 6, 3, 5, 7):
            place = at(t ^ d, td)
            block = ref.at[place, mine]
            drain(block, rv_a.at[k, d])
            if d == 1:
                for e in (2, 4, 6):
                    part_block = ref.at[place, left]
                    send(part_block, part_block, sd_a.at[k], rv_a.at[k, e + 1], shard(e))
            elif d % 2 == 0:
                part_block = ref.at[place, right]
                send(part_block, part_block, sd_a.at[k], rv_a.at[k, d + 1], shard(1))
            send(block, block, sf_a.at[k], rf_a.at[k, d], other)

    def await_blocks(k, ref):
        drain(ref.at[at(t, td), mine], ld_a.at[k])
        for d in range(nt):
            drain(ref.at[at(t ^ d, td), theirs], rf_a.at[k, d])

    forward_blocks(0, x_all)
    spread(1, og, o_all)
    await_blocks(0, x_all)

    half = tokens // 2

    hq = tq // 2
    low, high = pl.ds(0, hq), pl.ds(hq, hq)

    def sum_first(v, width):
        slot, w = lax.rem(v, SLOTS), pl.ds(0, width)
        for j, (dz, dy) in enumerate(((0, 0), (1, 0), (-1, 0), (2, 0), (0, 1))):
            keep[slot, j, :, w] = part[at(chip(dz, dy), tq), w]
        for j, (dz, dev) in enumerate(((2, over_y), (1, up_z), (-1, down_z))):
            s1[slot, j, :, w] = part[at(chip(dz, 1), tq), w].astype(BF)
            send(s1.at[slot, j, :, w], r1.at[slot, j, :, w], sd_1.at[slot], rv_1.at[slot], dev)

    def sum_second(v, width):
        slot, w = lax.rem(v, SLOTS), pl.ds(0, width)
        drain(r1.at[slot, :, :, w], rv_1.at[slot])
        s2[slot, 0, :, w] = (keep[slot, 3, :, w] + r1[slot, 0, :, w].astype(F32)).astype(BF)
        s2[slot, 1, :, w] = (
            keep[slot, 4, :, w] + r1[slot, 1, :, w].astype(F32) + r1[slot, 2, :, w].astype(F32)
        ).astype(BF)
        for rows, dev in ((low, down_z), (high, up_z)):
            send(s2.at[slot, 0, rows, w], r2.at[slot, 0, rows, w], sd_2.at[slot], rv_2.at[slot], dev)
        send(s2.at[slot, 1, :, w], r2.at[slot, 1, :, w], sd_2.at[slot], rv_3.at[slot], over_y)

    def sum_third(v, width):
        slot, w = lax.rem(v, SLOTS), pl.ds(0, width)
        drain(r2.at[slot, 0, :, w], rv_2.at[slot])
        s3[slot, 0, low, w] = (keep[slot, 2, low, w] + r2[slot, 0, low, w].astype(F32)).astype(BF)
        s3[slot, 0, high, w] = keep[slot, 2, high, w].astype(BF)
        s3[slot, 1, low, w] = keep[slot, 1, low, w].astype(BF)
        s3[slot, 1, high, w] = (keep[slot, 1, high, w] + r2[slot, 0, high, w].astype(F32)).astype(BF)
        for j, dev in enumerate((down_z, up_z)):
            send(s3.at[slot, j, :, w], r3.at[slot, j, :, w], sd_3.at[slot], rv_4.at[slot], dev)

    def sum_total(v, width):
        slot, w = lax.rem(v, SLOTS), pl.ds(0, width)
        drain(r2.at[slot, 1, :, w], rv_3.at[slot])
        drain(r3.at[slot, :, :, w], rv_4.at[slot])
        return (
            (keep[slot, 0, :, w] + r2[slot, 1, :, w].astype(F32))
            + (r3[slot, 0, :, w].astype(F32) + r3[slot, 1, :, w].astype(F32))
        )

    def sum_sent(v, width):
        slot, w = lax.rem(v, SLOTS), pl.ds(0, width)
        drain(s1.at[slot, :, :, w], sd_1.at[slot])
        drain(s2.at[slot, :, :, w], sd_2.at[slot])
        drain(s3.at[slot, :, :, w], sd_3.at[slot])

    def gather_first(ref, sd, rv):
        block = ref.at[at(q, tq)]
        for dev in (up_z, down_z, over_y):
            send(block, block, sd, rv.at[0], dev)

    def gather_second(ref, sd, rv, crossings):
        drain(ref.at[pl.ds(0, 3 * tq)], rv.at[0])
        below, above, beside = (chip(dz, dy) * tq for dz, dy in ((-1, 0), (1, 0), (0, 1)))
        moves = [(below, hq, up_z), (above + hq, hq, down_z)]
        if crossings == 3:
            moves += [(below, tq, over_y), (above, tq, over_y)]
        else:
            moves += [(beside, tq, up_z), (beside, tq, down_z)]
        for first, n, dev in moves:
            block = ref.at[pl.ds(pl.multiple_of(first, hq), n)]
            send(block, block, sd, rv.at[1], dev)

    def gather_third(ref, sd, rv, crossings):
        drain(ref.at[pl.ds(0, 3 * tq)], rv.at[1])
        if crossings == 3:
            moves = [(chip(-1, 1) * tq, hq, up_z), (chip(1, 1) * tq + hq, hq, down_z)]
        else:
            moves = [(chip(2, 0) * tq, tq, over_y)]
        for first, n, dev in moves:
            block = ref.at[pl.ds(pl.multiple_of(first, hq), n)]
            send(block, block, sd, rv.at[2], dev)

    def gather_done(ref, sd, rv):
        drain(ref.at[pl.ds(0, tq)], rv.at[2])
        drain(ref.at[pl.ds(0, 7 * tq)], sd)

    def fwd_partial(v):
        drain(w_gu.at[v, mine], ld_w.at[v])
        drain(w_gu.at[v, theirs], rv_w.at[v])

        @pl.loop(0, 2)
        def _(m):
            part[at(m, half), :] = dot_nn(x_all[at(m, half), :], w_gu[v])

        sum_first(v, 2 * CW)

    def fwd_sum(v):
        total = sum_total(v, 2 * CW)
        gu[v] = total
        gate, up = total[:, :CW], total[:, CW:]
        h_all[v, at(q, tq), :] = (gate * jax.nn.sigmoid(gate) * up).astype(BF)
        gather_first(h_all.at[v], sd_h.at[v], rv_h.at[v])

    def fwd_use(i):
        gather_done(h_all.at[i], sd_h.at[i], rv_h.at[i])

        @pl.loop(0, 4)
        def _(m):
            cols = pl.ds(pl.multiple_of(((oc * 2 + m) % 4) * hd, hd), hd)
            value = dot_nn(h_all[i], w_d[at(i, CW), cols])

            @pl.when(i == 0)
            def _():
                out_acc[:, cols] = value

            @pl.when(i > 0)
            def _():
                out_acc[:, cols] += value

            @pl.when((i == nc - 1) & (m < 2))
            def _():
                send(out_acc.at[:, cols], rx.at[0, m], s_x.at[0], r_x.at[0, m], other)

        s = lax.rem(i, 2)
        place = pl.ds(pl.multiple_of(c * fh + i * CW, CW), CW)

        @pl.when(i >= 2)
        def _():
            drain(st_d.at[s, :, mine], l_dg.at[s])
            drain(st_d.at[s, :, theirs], s_dg.at[s])

        st_d[s] = dot_tn(h_all[i], o_all[...]).astype(BF)
        pltpu.make_async_copy(st_d.at[s, :, mine], dg.at[place, :], l_dg.at[s]).start()
        send(st_d.at[s, :, theirs], dg.at[place, :], s_dg.at[s], r_dg, other)

    def bwd_partial(v):
        @pl.loop(0, 2)
        def _(m):
            part[at(m, half), pl.ds(0, CW)] = dot_nt(o_all[at(m, half), :], w_d[at(v - nc, CW), :])

        sum_first(v, CW)

    def bwd_sum(v):
        total = sum_total(v, CW)
        i = v - nc
        gate, up = gu[i, :, :CW], gu[i, :, CW:]
        sigma = jax.nn.sigmoid(gate)
        d_all[i, at(q, tq), :CW] = (total * up * sigma * (1.0 + gate * (1.0 - sigma))).astype(BF)
        d_all[i, at(q, tq), CW:] = (total * (gate * sigma)).astype(BF)
        gather_first(d_all.at[i], sd_dl.at[i], rv_dl.at[i])

    def bwd_use(i):
        gather_done(d_all.at[i], sd_dl.at[i], rv_dl.at[i])

        @pl.loop(0, 4)
        def _(m):
            cols = pl.ds(pl.multiple_of(((oc * 2 + m) % 4) * hd, hd), hd)
            value = dot_nt(d_all[i], w_gu[i, pl.ds(pl.multiple_of(((oc * 2 + m) % 4) * hd, hd), hd), :])

            @pl.when(i == 0)
            def _():
                in_acc[:, cols] = value

            @pl.when(i > 0)
            def _():
                in_acc[:, cols] += value

            @pl.when((i == nc - 1) & (m < 2))
            def _():
                send(in_acc.at[:, cols], rx.at[1, m], s_x.at[1], r_x.at[1, m], other)

        s = lax.rem(i, 2)
        place = pl.ds(pl.multiple_of(c * fh + i * CW, CW), CW)

        @pl.when(i >= 2)
        def _():
            drain(st_gu.at[s, mine], l_gu.at[s])
            drain(st_gu.at[s, theirs], s_gg.at[s])

        @pl.loop(0, 2)
        def _(m):
            st_gu[s, at(m, dd), :] = dot_nn(x_t[at(m, dd), :], d_all[i]).astype(BF)

        for j, (grad, r) in enumerate(((gg, 0), (ug, 1))):
            lanes = pl.ds(j * CW, CW)
            pltpu.make_async_copy(st_gu.at[s, mine, lanes], grad.at[:, place], l_gu.at[s]).start()
            send(st_gu.at[s, theirs, lanes], grad.at[:, place], s_gg.at[s], r_gg.at[r], other)

    x, h = t // 2, t % 2
    left = pl.ds(pl.multiple_of(c * dd, hd), hd)
    right = pl.ds(pl.multiple_of(c * dd + hd, hd), hd)

    def reduce_left(k, acc):
        drain(rx.at[k, 0], r_x.at[k, 0])
        for m in range(4):
            strip = at(x ^ ((m + 1) % 4), 2 * td)
            value = acc[strip, left] + rx[k, 0, strip, :]
            if m < 3:
                ta[k, m] = value.astype(BF)
                send(ta.at[k, m], ra.at[k, m], s_a.at[k], r_a.at[k], shard(2 * (m + 1)))
            else:
                rx[k, 0, strip, :] = value

    def reduce_right(k, acc):
        drain(rx.at[k, 1], r_x.at[k, 1])
        for m in range(4):
            place = at(m * 2 + 1 - h, td)
            tb[k, m] = (acc[place, right] + rx[k, 1, place, :]).astype(BF)
        send(tb.at[k], rb.at[k], s_b.at[k], r_b.at[k], shard(1))
        for m in range(4):
            place = at(m * 2 + h, td)
            rx[k, 1, place, :] = acc[place, right] + rx[k, 1, place, :]

    def reduce_cross(k):
        drain(rb.at[k], r_b.at[k])
        for m in range(4):
            over = x ^ ((m + 1) % 4)
            place = at(over * 2 + h, td)
            value = rx[k, 1, place, :] + rb[k, over].astype(F32)
            if m < 3:
                tc[k, m] = value.astype(BF)
                send(tc.at[k, m], rc.at[k, m], s_c.at[k], r_c.at[k], shard(2 * (m + 1)))
            else:
                rx[k, 1, place, :] = value
        drain(ra.at[k], r_a.at[k])
        for e in (1, 0):
            block = rx.at[k, 0, at(t ^ e, td)]
            total = block[...]
            for d in range(3):
                total = total + ra[k, d, at(h ^ e, td), :].astype(F32)
            block[...] = total
            if e == 1:
                send(block, ry.at[k], s_y.at[k], r_y.at[k], shard(1))

    def reduce_done(k, result):
        drain(rc.at[k], r_c.at[k])
        total = rx[k, 1, at(t, td), :]
        for d in range(3):
            total = total + rc[k, d].astype(F32)
        to[k, :, hd:] = total.astype(BF)
        drain(ry.at[k], r_y.at[k])
        to[k, :, :hd] = (rx[k, 0, at(t, td), :] + ry[k]).astype(BF)
        pltpu.make_async_copy(to.at[k], result, l_o.at[k]).start()
        drain(rx.at[k], s_x.at[k])
        drain(ta.at[k], s_a.at[k])
        drain(tb.at[k], s_b.at[k])
        drain(tc.at[k], s_c.at[k])
        drain(ry.at[k], s_y.at[k])

    def fwd_second(i):
        gather_second(h_all.at[i], sd_h.at[i], rv_h.at[i], 3)
        sum_sent(i, 2 * CW)

    def bwd_second(i):
        gather_second(d_all.at[i - nc], sd_dl.at[i - nc], rv_dl.at[i - nc], 2)
        sum_sent(i, CW)

    use = LAG[5]

    def stage(v, lag, fwd, bwd):
        i = v - lag
        pl.when((i >= 0) & (i < nc))(lambda: fwd(i))
        pl.when((i >= nc) & (i < 2 * nc))(lambda: bwd(i))

    @pl.loop(0, 2 * nc + use)
    def _(v):
        stage(
            v, LAG[4],
            lambda i: gather_third(h_all.at[i], sd_h.at[i], rv_h.at[i], 3),
            lambda i: gather_third(d_all.at[i - nc], sd_dl.at[i - nc], rv_dl.at[i - nc], 2),
        )
        stage(
            v, LAG[3],
            fwd_second,
            bwd_second,
        )
        stage(v, LAG[2], fwd_sum, bwd_sum)
        stage(v, LAG[1], lambda i: sum_third(i, 2 * CW), lambda i: sum_third(i, CW))
        stage(v, LAG[0], lambda i: sum_second(i, 2 * CW), lambda i: sum_second(i, CW))
        stage(v, 0, fwd_partial, bwd_partial)

        @pl.when(v == 3)
        def _():
            forward_blocks(1, o_all)
            drain(w_d.at[:, mine], ld_d)
            drain(w_d.at[:, theirs], rv_d)

            @pl.loop(0, nt)
            def _(j):
                x_t[:, at(j, td)] = x_all[at(j, td), :].T

        @pl.when(v == use)
        def _():
            await_blocks(1, o_all)

        stage(v, use, fwd_use, lambda i: bwd_use(i - nc))

        @pl.when(v == nc + use)
        def _():
            reduce_left(0, out_acc)
            reduce_right(0, out_acc)

        @pl.when(v == nc + use + 4)
        def _():
            reduce_cross(0)

        @pl.when(v == nc + use + 7)
        def _():
            reduce_done(0, out)

    reduce_left(1, in_acc)
    reduce_right(1, in_acc)
    reduce_cross(1)
    reduce_done(1, ig)

    for s in range(2):
        drain(st_d.at[s, :, mine], l_dg.at[s])
        drain(st_d.at[s, :, theirs], s_dg.at[s])
        drain(st_gu.at[s, mine], l_gu.at[s])
        drain(st_gu.at[s, theirs], s_gg.at[s])
        drain(to.at[s], l_o.at[s])
    partner = at(oc, fh)
    drain(dg.at[partner, :], r_dg)
    drain(gg.at[:, partner], r_gg.at[0])
    drain(ug.at[:, partner], r_gg.at[1])
    drain(w_gu.at[:, mine], sd_w)
    drain(w_d.at[:, mine], sd_d)
    for k, ref in enumerate((x_all, o_all)):
        drain(ref.at[:, pl.ds(0, dd)], sd_a.at[k])
        drain(ref.at[pl.ds(0, (nt - 1) * td), pl.ds(0, dd)], sf_a.at[k])


PIECES = 4


def hand_over(*refs):
    srcs, dsts, holds, (ins, outs) = refs[:5], refs[5:10], refs[10:15], refs[15:]
    pieces = []
    for j in (2, 3, 4, 0, 1):
        n = srcs[j].shape[0] // PIECES
        for p in range(PIECES):
            place = pl.ds(p * n, n)
            pieces.append((
                pltpu.make_async_copy(srcs[j].at[place], holds[j].at[place], ins.at[j, p]),
                pltpu.make_async_copy(holds[j].at[place], dsts[j].at[place], outs.at[j, p]),
            ))
    for copy, _ in pieces:
        copy.start()
    for copy, leave in pieces:
        copy.wait()
        leave.start()
    for _, leave in pieces:
        leave.wait()


def per_device(tokens, gate_weight, up_weight, down_weight, out_grad):
    nt = lax.axis_size("tensor")
    td, dd = tokens.shape
    ff = gate_weight.shape[1]
    fh = ff // 2
    nc = fh // CW
    n = nt * td
    tq = n // (2 * NZ)
    d2, hd = 2 * dd, dd // 2
    vmem = pltpu.VMEM
    dma = pltpu.SemaphoreType.DMA
    anywhere = pl.BlockSpec(memory_space=pl.ANY)
    results = pl.pallas_call(
        functools.partial(kernel, (nt, td, dd, tq, fh, nc)),
        name="swiglu",
        out_shape=(
            jax.ShapeDtypeStruct((td, dd), BF),
            jax.ShapeDtypeStruct((td, dd), BF),
            jax.ShapeDtypeStruct((dd, ff), BF),
            jax.ShapeDtypeStruct((dd, ff), BF),
            jax.ShapeDtypeStruct((ff, dd), BF),
        ),
        in_specs=[anywhere] * 5,
        out_specs=(anywhere,) * 5,
        scratch_shapes=[
            vmem((nc, d2, 2 * CW), BF),
            vmem((fh, d2), BF),
            vmem((n, d2), BF),
            vmem((d2, n), BF),
            vmem((n, d2), BF),
            vmem((nc, n, CW), BF),
            vmem((nc, n, 2 * CW), BF),
            vmem((n, d2), F32),
            vmem((n, d2), F32),
            vmem((n, 2 * CW), F32),
            vmem((SLOTS, 5, tq, 2 * CW), F32),
            vmem((SLOTS, 3, tq, 2 * CW), BF),
            vmem((SLOTS, 2, tq, 2 * CW), BF),
            vmem((SLOTS, 2, tq, 2 * CW), BF),
            vmem((SLOTS, 3, tq, 2 * CW), BF),
            vmem((SLOTS, 2, tq, 2 * CW), BF),
            vmem((SLOTS, 2, tq, 2 * CW), BF),
            vmem((nc, tq, 2 * CW), F32),
            vmem((2, CW, d2), BF),
            vmem((2, d2, 2 * CW), BF),
            vmem((2, 2, n, hd), F32),
            vmem((2, td, hd), F32),
            vmem((2, 3, 2 * td, hd), BF),
            vmem((2, 3, 2 * td, hd), BF),
            vmem((2, 4, td, hd), BF),
            vmem((2, 4, td, hd), BF),
            vmem((2, 3, td, hd), BF),
            vmem((2, 3, td, hd), BF),
            vmem((2, td, dd), BF),
            dma((nc,)), dma((nc,)), dma,
            dma, dma, dma,
            dma((2,)), dma((2, nt)), dma((2,)), dma((2, nt)), dma((2,)),
            dma((SLOTS,)), dma((SLOTS,)), dma((SLOTS,)),
            dma((SLOTS,)), dma((SLOTS,)), dma((SLOTS,)), dma((SLOTS,)),
            dma((nc,)), dma((nc, 3)), dma((nc,)), dma((nc, 3)),
            dma((2,)), dma((2,)), dma,
            dma((2,)), dma((2,)), dma((2,)),
            dma((2,)), dma((2, 2)), dma((2,)), dma((2,)), dma((2,)), dma((2,)), dma((2,)), dma((2,)), dma((2,)), dma((2,)), dma((2,)),
        ],
        compiler_params=pltpu.CompilerParams(
            collective_id=0, has_side_effects=True, vmem_limit_bytes=63 * 1024 * 1024
        ),
        cost_estimate=pl.CostEstimate(flops=18 * n * d2 * fh, bytes_accessed=6 * ff * dd * 2, transcendentals=0),
    )(tokens, gate_weight, up_weight, down_weight, out_grad)
    return pl.pallas_call(
        hand_over,
        name="hand_over",
        out_shape=tuple(jax.ShapeDtypeStruct(r.shape, r.dtype) for r in results),
        in_specs=[anywhere] * 5,
        out_specs=(anywhere,) * 5,
        scratch_shapes=[vmem(r.shape, r.dtype) for r in results] + [dma((5, PIECES)), dma((5, PIECES))],
        compiler_params=pltpu.CompilerParams(vmem_limit_bytes=60 * 1024 * 1024),
    )(*results)


def solution(mesh):
    act, wide, tall = P("tensor", "pipe"), P("pipe", "tensor"), P("tensor", "pipe")
    return jax.shard_map(
        per_device,
        mesh=mesh,
        in_specs=(act, wide, wide, tall, act),
        out_specs=(act, act, wide, wide, tall),
        check_vma=False,
    )
```

time: 331 us -> 219 us (0.66); the launches traced: 328 us -> 219 us
  Pallas kernels: 315 us -> 218 us
  local copies, waits for them, and re-layouts: 12.6 us -> 0 us
    pallas_call x1 -> x2, Pallas kernels: 315 us -> 218 us  [the longest x1 210 us: per_device(): pl.pallas_call(functools.partial(kernel, (nt, td, dd, tq, fh, nc)), name=...]
    unnamed x9 -> x0, local copies, waits for them, and re-layouts: 12.6 us -> none
where the time goes in v2:
time: 219 us
  Pallas kernels  218 us (100%)
    pallas_call x1, Pallas kernels, per_device(): pl.pallas_call(functools.partial(kernel, (nt, td, dd, tq, fh, nc)), name=...  210 us
    pallas_call x1, Pallas kernels, per_device(): pl.pallas_call(hand_over, name='hand_over', out_shape=tuple((jax.ShapeDty...  8.77 us

profile of v2, /device:TPU:1, one launch (start us, length us, event | category | flops | bytes accessed | tf_op | source)
XLA Modules:
  0.0 219.1 jit_solution(2922027179938418229)
XLA Ops:
  0.6 209.7 %swiglu.1 = (bf16[128,512]{1,0:T(8,128)(2,1)}, bf16[128,512]{1,0:T(8,128)(2,1)}, bf16[512,3584]{1,0:T(8,128)(2,1)}, bf16[512,3584]{1,0:T(8,128)(2,1)}, bf16[3584,512]{1,0:T(8,128)(2,1)}) custom-call(bf16[128,512]{1,0:T(8,128)(2,1)} %tok.1, bf16[512,3584]{1,0:T(8,128)(2,1)} %wg.1, bf16[512,3584]{1,0:T(8,128)(2,1)} %wu.1, bf16[3584,512]{1,0:T(8,128)(2,1)} %wd.1, ...), custom_call_target="tpu_custom_call" | custom-call | flops 33822867456 | bytes 22020096 | tf_op jit(solution)/shard_map/swiglu/pallas_call | solution.py:490
  210.3 8.8 %hand_over.1 = (bf16[128,512]{1,0:T(8,128)(2,1)}, bf16[128,512]{1,0:T(8,128)(2,1)}, bf16[512,3584]{1,0:T(8,128)(2,1)}, bf16[512,3584]{1,0:T(8,128)(2,1)}, bf16[3584,512]{1,0:T(8,128)(2,1)}) custom-call(bf16[128,512]{1,0:T(8,128)(2,1)} %get-tuple-element.10.refs_0_, bf16[128,512]{1,0:T(8,128)(2,1)} %get-tuple-element.11.refs_1_, ...), custom_call_target="tpu_custom_call" | custom-call | tf_op jit(solution)/shard_map/hand_over/pallas_call | solution.py:547

commit v3 on v2

--- a/solution.py
+++ b/solution.py
@@ -13,7 +13,8 @@
 NZ = 4
 CW = 128
 SLOTS = 8
-LAG = (2, 4, 6, 8, 10, 12)
+LAG = (2, 4, 6, 8, 10, 11)
+LATE = (3, 2)
 
 
 def dot_nn(a, b):
@@ -39,7 +40,7 @@
     w_gu, w_d, x_all, x_t, o_all, h_all, d_all, out_acc, in_acc, part,
     keep, s1, s2, s3, r1, r2, r3, gu, st_d, st_gu, rx, ry, ta, ra, tb, rb, tc, rc, to,
     ld_w, rv_w, sd_w, ld_d, rv_d, sd_d, ld_a, rv_a, sd_a, rf_a, sf_a,
-    sd_1, sd_2, sd_3, rv_1, rv_2, rv_3, rv_4, sd_h, rv_h, sd_dl, rv_dl,
+    free, sd_1, sd_2, sd_3, rv_1, rv_2, rv_3, rv_4, sd_h, rv_h, sd_dl, rv_dl,
     l_dg, s_dg, r_dg, l_gu, s_gg, r_gg, s_x, r_x, s_a, r_a, s_b, r_b, s_c, r_c, s_y, r_y, l_o,
 ):
     nt, td, dd, tq, fh, nc = dims
@@ -78,12 +79,18 @@
     pl.semaphore_signal(barrier, inc=1, device_id=other, device_id_type=MESH)
     pl.semaphore_wait(barrier, 8)
 
+    hd = dd // 2
+    left = pl.ds(pl.multiple_of(c * dd, hd), hd)
+    right = pl.ds(pl.multiple_of(c * dd + hd, hd), hd)
+
     def spread(k, src, dst):
-        block = dst.at[at(t, td), mine]
+        place = at(t, td)
+        for d, first in ((2, False), (4, False), (6, False), (1, True), (2, True), (4, True), (6, True), (1, False)):
+            cols, j = (left, 0) if first else (right, 1)
+            send(src.at[:, pl.ds(j * hd, hd)], dst.at[place, cols], sd_a.at[k], rv_a.at[k, d, j], shard(d))
+        block = dst.at[place, mine]
         pltpu.make_async_copy(src, block, ld_a.at[k]).start()
-        for d in (1, 2, 4, 6):
-            send(src, block, sd_a.at[k], rv_a.at[k, d], shard(d))
-        send(src, block, sd_a.at[k], rf_a.at[k, 0], other)
+        send(src, block, sd_a.at[k], rf_a.at[k, 0, 0], other)
 
     spread(0, tok, x_all)
 
@@ -99,28 +106,26 @@
     pltpu.make_async_copy(wd.at[at(c, fh), :], w_d.at[:, mine], ld_d).start()
     send(wd.at[at(oc, fh), :], w_d.at[:, mine], sd_d, rv_d, other)
 
-    hd = dd // 2
-
     def forward_blocks(k, ref):
-        left = pl.ds(pl.multiple_of(c * dd, hd), hd)
-        right = pl.ds(pl.multiple_of(c * dd + hd, hd), hd)
-        for d in (1, 2, 4, 6, 3, 5, 7):
-            place = at(t ^ d, td)
-            block = ref.at[place, mine]
-            drain(block, rv_a.at[k, d])
-            if d == 1:
+        order = [(1, 0), (2, 1), (4, 1), (6, 1), (2, 0), (4, 0), (6, 0), (1, 1)]
+        order += [(3, 0), (3, 1), (5, 0), (5, 1), (7, 0), (7, 1)]
+        for d, j in order:
+            block = ref.at[at(t ^ d, td), (left, right)[j]]
+            drain(block, rv_a.at[k, d, j])
+            if (d, j) == (1, 0):
                 for e in (2, 4, 6):
-                    part_block = ref.at[place, left]
-                    send(part_block, part_block, sd_a.at[k], rv_a.at[k, e + 1], shard(e))
-            elif d % 2 == 0:
-                part_block = ref.at[place, right]
-                send(part_block, part_block, sd_a.at[k], rv_a.at[k, d + 1], shard(1))
-            send(block, block, sf_a.at[k], rf_a.at[k, d], other)
+                    send(block, block, sd_a.at[k], rv_a.at[k, e + 1, j], shard(e))
+            elif d in (2, 4, 6) and j == 1:
+                send(block, block, sd_a.at[k], rv_a.at[k, d + 1, j], shard(1))
+            send(block, block, sf_a.at[k], rf_a.at[k, d, j], other)
 
     def await_blocks(k, ref):
         drain(ref.at[at(t, td), mine], ld_a.at[k])
-        for d in range(nt):
-            drain(ref.at[at(t ^ d, td), theirs], rf_a.at[k, d])
+        drain(ref.at[at(t, td), theirs], rf_a.at[k, 0, 0])
+        for d in range(1, nt):
+            for j in range(2):
+                cols = pl.ds(pl.multiple_of(oc * dd + j * hd, hd), hd)
+                drain(ref.at[at(t ^ d, td), cols], rf_a.at[k, d, j])
 
     forward_blocks(0, x_all)
     spread(1, og, o_all)
@@ -133,6 +138,12 @@
 
     def sum_first(v, width):
         slot, w = lax.rem(v, SLOTS), pl.ds(0, width)
+
+        @pl.when(v >= SLOTS)
+        def _():
+            for j in range(3):
+                pl.semaphore_wait(free.at[j], 1)
+
         for j, (dz, dy) in enumerate(((0, 0), (1, 0), (-1, 0), (2, 0), (0, 1))):
             keep[slot, j, :, w] = part[at(chip(dz, dy), tq), w]
         for j, (dz, dev) in enumerate(((2, over_y), (1, up_z), (-1, down_z))):
@@ -164,10 +175,16 @@
         slot, w = lax.rem(v, SLOTS), pl.ds(0, width)
         drain(r2.at[slot, 1, :, w], rv_3.at[slot])
         drain(r3.at[slot, :, :, w], rv_4.at[slot])
-        return (
-            (keep[slot, 0, :, w] + r2[slot, 1, :, w].astype(F32))
-            + (r3[slot, 0, :, w].astype(F32) + r3[slot, 1, :, w].astype(F32))
+        total = (keep[slot, 0, :, w] + r2[slot, 1, :, w].astype(F32)) + (
+            r3[slot, 0, :, w].astype(F32) + r3[slot, 1, :, w].astype(F32)
         )
+
+        @pl.when(v < 2 * nc - SLOTS)
+        def _():
+            for j, dev in enumerate((down_z, up_z, over_y)):
+                pl.semaphore_signal(free.at[j], inc=1, device_id=dev, device_id_type=MESH)
+
+        return total
 
     def sum_sent(v, width):
         slot, w = lax.rem(v, SLOTS), pl.ds(0, width)
@@ -206,6 +223,12 @@
         drain(ref.at[pl.ds(0, tq)], rv.at[2])
         drain(ref.at[pl.ds(0, 7 * tq)], sd)
 
+    def col_block(m):
+        return pl.ds(pl.multiple_of(((oc * 2 + 1 - m % 2 + m // 2 * 2) % 4) * hd, hd), hd)
+
+    def h_of(i):
+        return h_all.at[i // 2, :, at(i % 2, CW)]
+
     def fwd_partial(v):
         drain(w_gu.at[v, mine], ld_w.at[v])
         drain(w_gu.at[v, theirs], rv_w.at[v])
@@ -220,38 +243,41 @@
         total = sum_total(v, 2 * CW)
         gu[v] = total
         gate, up = total[:, :CW], total[:, CW:]
-        h_all[v, at(q, tq), :] = (gate * jax.nn.sigmoid(gate) * up).astype(BF)
-        gather_first(h_all.at[v], sd_h.at[v], rv_h.at[v])
+        block = h_of(v).at[at(q, tq)]
+        block[...] = (gate * jax.nn.sigmoid(gate) * up).astype(BF)
+        gather_first(h_of(v), sd_h.at[v], rv_h.at[v])
 
     def fwd_use(i):
-        gather_done(h_all.at[i], sd_h.at[i], rv_h.at[i])
-
+        gather_done(h_of(i), sd_h.at[i], rv_h.at[i])
+        pl.when(i % 2 == 1)(lambda: fwd_pair(i // 2))
+
+    def fwd_pair(p):
         @pl.loop(0, 4)
         def _(m):
-            cols = pl.ds(pl.multiple_of(((oc * 2 + m) % 4) * hd, hd), hd)
-            value = dot_nn(h_all[i], w_d[at(i, CW), cols])
-
-            @pl.when(i == 0)
+            cols = col_block(m)
+            value = dot_nn(h_all[p], w_d[at(p, 2 * CW), cols])
+
+            @pl.when(p == 0)
             def _():
                 out_acc[:, cols] = value
 
-            @pl.when(i > 0)
+            @pl.when(p > 0)
             def _():
                 out_acc[:, cols] += value
 
-            @pl.when((i == nc - 1) & (m < 2))
+            @pl.when((p == nc // 2 - 1) & (m < 2))
             def _():
                 send(out_acc.at[:, cols], rx.at[0, m], s_x.at[0], r_x.at[0, m], other)
 
-        s = lax.rem(i, 2)
-        place = pl.ds(pl.multiple_of(c * fh + i * CW, CW), CW)
-
-        @pl.when(i >= 2)
+        s = lax.rem(p, 2)
+        place = pl.ds(pl.multiple_of(c * fh + p * (2 * CW), CW), 2 * CW)
+
+        @pl.when(p >= 2)
         def _():
             drain(st_d.at[s, :, mine], l_dg.at[s])
             drain(st_d.at[s, :, theirs], s_dg.at[s])
 
-        st_d[s] = dot_tn(h_all[i], o_all[...]).astype(BF)
+        st_d[s] = dot_tn(h_all[p], o_all[...]).astype(BF)
         pltpu.make_async_copy(st_d.at[s, :, mine], dg.at[place, :], l_dg.at[s]).start()
         send(st_d.at[s, :, theirs], dg.at[place, :], s_dg.at[s], r_dg, other)
 
@@ -276,8 +302,8 @@
 
         @pl.loop(0, 4)
         def _(m):
-            cols = pl.ds(pl.multiple_of(((oc * 2 + m) % 4) * hd, hd), hd)
-            value = dot_nt(d_all[i], w_gu[i, pl.ds(pl.multiple_of(((oc * 2 + m) % 4) * hd, hd), hd), :])
+            cols = col_block(m)
+            value = dot_nt(d_all[i], w_gu[i, cols, :])
 
             @pl.when(i == 0)
             def _():
@@ -291,6 +317,9 @@
             def _():
                 send(in_acc.at[:, cols], rx.at[1, m], s_x.at[1], r_x.at[1, m], other)
 
+        pl.when(i < nc - sum(LATE))(lambda: weight_grads(i))
+
+    def weight_grads(i):
         s = lax.rem(i, 2)
         place = pl.ds(pl.multiple_of(c * fh + i * CW, CW), CW)
 
@@ -309,44 +338,42 @@
             send(st_gu.at[s, theirs, lanes], grad.at[:, place], s_gg.at[s], r_gg.at[r], other)
 
     x, h = t // 2, t % 2
-    left = pl.ds(pl.multiple_of(c * dd, hd), hd)
-    right = pl.ds(pl.multiple_of(c * dd + hd, hd), hd)
 
     def reduce_left(k, acc):
-        drain(rx.at[k, 0], r_x.at[k, 0])
+        drain(rx.at[k, 1], r_x.at[k, 1])
         for m in range(4):
             strip = at(x ^ ((m + 1) % 4), 2 * td)
-            value = acc[strip, left] + rx[k, 0, strip, :]
+            value = acc[strip, left] + rx[k, 1, strip, :]
             if m < 3:
                 ta[k, m] = value.astype(BF)
                 send(ta.at[k, m], ra.at[k, m], s_a.at[k], r_a.at[k], shard(2 * (m + 1)))
             else:
-                rx[k, 0, strip, :] = value
+                rx[k, 1, strip, :] = value
 
     def reduce_right(k, acc):
-        drain(rx.at[k, 1], r_x.at[k, 1])
+        drain(rx.at[k, 0], r_x.at[k, 0])
         for m in range(4):
             place = at(m * 2 + 1 - h, td)
-            tb[k, m] = (acc[place, right] + rx[k, 1, place, :]).astype(BF)
+            tb[k, m] = (acc[place, right] + rx[k, 0, place, :]).astype(BF)
         send(tb.at[k], rb.at[k], s_b.at[k], r_b.at[k], shard(1))
         for m in range(4):
             place = at(m * 2 + h, td)
-            rx[k, 1, place, :] = acc[place, right] + rx[k, 1, place, :]
+            rx[k, 0, place, :] = acc[place, right] + rx[k, 0, place, :]
 
     def reduce_cross(k):
         drain(rb.at[k], r_b.at[k])
         for m in range(4):
             over = x ^ ((m + 1) % 4)
             place = at(over * 2 + h, td)
-            value = rx[k, 1, place, :] + rb[k, over].astype(F32)
+            value = rx[k, 0, place, :] + rb[k, over].astype(F32)
             if m < 3:
                 tc[k, m] = value.astype(BF)
                 send(tc.at[k, m], rc.at[k, m], s_c.at[k], r_c.at[k], shard(2 * (m + 1)))
             else:
-                rx[k, 1, place, :] = value
+                rx[k, 0, place, :] = value
         drain(ra.at[k], r_a.at[k])
         for e in (1, 0):
-            block = rx.at[k, 0, at(t ^ e, td)]
+            block = rx.at[k, 1, at(t ^ e, td)]
             total = block[...]
             for d in range(3):
                 total = total + ra[k, d, at(h ^ e, td), :].astype(F32)
@@ -356,12 +383,12 @@
 
     def reduce_done(k, result):
         drain(rc.at[k], r_c.at[k])
-        total = rx[k, 1, at(t, td), :]
+        total = rx[k, 0, at(t, td), :]
         for d in range(3):
             total = total + rc[k, d].astype(F32)
         to[k, :, hd:] = total.astype(BF)
         drain(ry.at[k], r_y.at[k])
-        to[k, :, :hd] = (rx[k, 0, at(t, td), :] + ry[k]).astype(BF)
+        to[k, :, :hd] = (rx[k, 1, at(t, td), :] + ry[k]).astype(BF)
         pltpu.make_async_copy(to.at[k], result, l_o.at[k]).start()
         drain(rx.at[k], s_x.at[k])
         drain(ta.at[k], s_a.at[k])
@@ -369,14 +396,6 @@
         drain(tc.at[k], s_c.at[k])
         drain(ry.at[k], s_y.at[k])
 
-    def fwd_second(i):
-        gather_second(h_all.at[i], sd_h.at[i], rv_h.at[i], 3)
-        sum_sent(i, 2 * CW)
-
-    def bwd_second(i):
-        gather_second(d_all.at[i - nc], sd_dl.at[i - nc], rv_dl.at[i - nc], 2)
-        sum_sent(i, CW)
-
     use = LAG[5]
 
     def stage(v, lag, fwd, bwd):
@@ -386,41 +405,42 @@
 
     @pl.loop(0, 2 * nc + use)
     def _(v):
+        stage(v, 0, fwd_partial, bwd_partial)
         stage(
             v, LAG[4],
-            lambda i: gather_third(h_all.at[i], sd_h.at[i], rv_h.at[i], 3),
+            lambda i: gather_third(h_of(i), sd_h.at[i], rv_h.at[i], 3),
             lambda i: gather_third(d_all.at[i - nc], sd_dl.at[i - nc], rv_dl.at[i - nc], 2),
         )
         stage(
             v, LAG[3],
-            fwd_second,
-            bwd_second,
+            lambda i: gather_second(h_of(i), sd_h.at[i], rv_h.at[i], 3),
+            lambda i: gather_second(d_all.at[i - nc], sd_dl.at[i - nc], rv_dl.at[i - nc], 2),
         )
         stage(v, LAG[2], fwd_sum, bwd_sum)
+        stage(v, LAG[2] + 1, lambda i: sum_sent(i, 2 * CW), lambda i: sum_sent(i, CW))
         stage(v, LAG[1], lambda i: sum_third(i, 2 * CW), lambda i: sum_third(i, CW))
         stage(v, LAG[0], lambda i: sum_second(i, 2 * CW), lambda i: sum_second(i, CW))
-        stage(v, 0, fwd_partial, bwd_partial)
-
-        @pl.when(v == 3)
+
+        @pl.when(v == use - 4)
         def _():
             forward_blocks(1, o_all)
+
+        @pl.when(v == use)
+        def _():
+            await_blocks(1, o_all)
             drain(w_d.at[:, mine], ld_d)
             drain(w_d.at[:, theirs], rv_d)
 
-            @pl.loop(0, nt)
-            def _(j):
-                x_t[:, at(j, td)] = x_all[at(j, td), :].T
-
-        @pl.when(v == use)
-        def _():
-            await_blocks(1, o_all)
+        @pl.when((v >= nc) & (v < nc + nt))
+        def _():
+            x_t[:, at(v - nc, td)] = x_all[at(v - nc, td), :].T
 
         stage(v, use, fwd_use, lambda i: bwd_use(i - nc))
 
         @pl.when(v == nc + use)
         def _():
+            reduce_right(0, out_acc)
             reduce_left(0, out_acc)
-            reduce_right(0, out_acc)
 
         @pl.when(v == nc + use + 4)
         def _():
@@ -430,9 +450,11 @@
         def _():
             reduce_done(0, out)
 
+    reduce_right(1, in_acc)
     reduce_left(1, in_acc)
-    reduce_right(1, in_acc)
+    pl.loop(nc - sum(LATE), nc - LATE[1])(weight_grads)
     reduce_cross(1)
+    pl.loop(nc - LATE[1], nc)(weight_grads)
     reduce_done(1, ig)
 
     for s in range(2):
@@ -505,7 +527,7 @@
             vmem((n, d2), BF),
             vmem((d2, n), BF),
             vmem((n, d2), BF),
-            vmem((nc, n, CW), BF),
+            vmem((nc // 2, n, 2 * CW), BF),
             vmem((nc, n, 2 * CW), BF),
             vmem((n, d2), F32),
             vmem((n, d2), F32),
@@ -518,7 +540,7 @@
             vmem((SLOTS, 2, tq, 2 * CW), BF),
             vmem((SLOTS, 2, tq, 2 * CW), BF),
             vmem((nc, tq, 2 * CW), F32),
-            vmem((2, CW, d2), BF),
+            vmem((2, 2 * CW, d2), BF),
             vmem((2, d2, 2 * CW), BF),
             vmem((2, 2, n, hd), F32),
             vmem((2, td, hd), F32),
@@ -531,7 +553,8 @@
             vmem((2, td, dd), BF),
             dma((nc,)), dma((nc,)), dma,
             dma, dma, dma,
-            dma((2,)), dma((2, nt)), dma((2,)), dma((2, nt)), dma((2,)),
+            dma((2,)), dma((2, nt, 2)), dma((2,)), dma((2, nt, 2)), dma((2,)),
+            pltpu.SemaphoreType.REGULAR((3,)),
             dma((SLOTS,)), dma((SLOTS,)), dma((SLOTS,)),
             dma((SLOTS,)), dma((SLOTS,)), dma((SLOTS,)), dma((SLOTS,)),
             dma((nc,)), dma((nc, 3)), dma((nc,)), dma((nc, 3)),

time: 219 us -> 208 us (0.950)
  Pallas kernels: 218 us -> 207 us
    pallas_call x1, Pallas kernels: 210 us -> 198 us  [per_device(): pl.pallas_call(functools.partial(kernel, (nt, td, dd, tq, fh, nc)), name=...]
where the time goes in v3:
time: 208 us
  Pallas kernels  207 us (100%)
    pallas_call x1, Pallas kernels, per_device(): pl.pallas_call(functools.partial(kernel, (nt, td, dd, tq, fh, nc)), name=...  198 us
    pallas_call x1, Pallas kernels, per_device(): pl.pallas_call(hand_over, name='hand_over', out_shape=tuple((jax.ShapeDty...  8.77 us

profile of v3, /device:TPU:1, one launch (start us, length us, event | category | flops | bytes accessed | tf_op | source)
XLA Modules:
  0.0 207.6 jit_solution(9009485524094513640)
XLA Ops:
  0.6 198.2 %swiglu.1 = (bf16[128,512]{1,0:T(8,128)(2,1)}, bf16[128,512]{1,0:T(8,128)(2,1)}, bf16[512,3584]{1,0:T(8,128)(2,1)}, bf16[512,3584]{1,0:T(8,128)(2,1)}, bf16[3584,512]{1,0:T(8,128)(2,1)}) custom-call(bf16[128,512]{1,0:T(8,128)(2,1)} %tok.1, bf16[512,3584]{1,0:T(8,128)(2,1)} %wg.1, bf16[512,3584]{1,0:T(8,128)(2,1)} %wu.1, bf16[3584,512]{1,0:T(8,128)(2,1)} %wd.1, ...), custom_call_target="tpu_custom_call" | custom-call | flops 33822867456 | bytes 22020096 | tf_op jit(solution)/shard_map/swiglu/pallas_call | solution.py:512
  198.9 8.8 %hand_over.1 = (bf16[128,512]{1,0:T(8,128)(2,1)}, bf16[128,512]{1,0:T(8,128)(2,1)}, bf16[512,3584]{1,0:T(8,128)(2,1)}, bf16[512,3584]{1,0:T(8,128)(2,1)}, bf16[3584,512]{1,0:T(8,128)(2,1)}) custom-call(bf16[128,512]{1,0:T(8,128)(2,1)} %get-tuple-element.10.refs_0_, bf16[128,512]{1,0:T(8,128)(2,1)} %get-tuple-element.11.refs_1_, ...), custom_call_target="tpu_custom_call" | custom-call | tf_op jit(solution)/shard_map/hand_over/pallas_call | solution.py:570

commit v4 on v3

--- a/solution.py
+++ b/solution.py
@@ -112,10 +112,10 @@
         for d, j in order:
             block = ref.at[at(t ^ d, td), (left, right)[j]]
             drain(block, rv_a.at[k, d, j])
-            if (d, j) == (1, 0):
+            if d == 1 and (j == 0 or k == 1):
                 for e in (2, 4, 6):
                     send(block, block, sd_a.at[k], rv_a.at[k, e + 1, j], shard(e))
-            elif d in (2, 4, 6) and j == 1:
+            elif d in (2, 4, 6) and j == 1 and k == 0:
                 send(block, block, sd_a.at[k], rv_a.at[k, d + 1, j], shard(1))
             send(block, block, sf_a.at[k], rf_a.at[k, d, j], other)
 
@@ -398,6 +398,10 @@
 
     use = LAG[5]
 
+    def some(i, hop):
+        for crossings, chosen in ((3, i % 4 == 1), (2, i % 4 != 1)):
+            pl.when(chosen)(functools.partial(hop, d_all.at[i], sd_dl.at[i], rv_dl.at[i], crossings))
+
     def stage(v, lag, fwd, bwd):
         i = v - lag
         pl.when((i >= 0) & (i < nc))(lambda: fwd(i))
@@ -405,18 +409,18 @@
 
     @pl.loop(0, 2 * nc + use)
     def _(v):
-        stage(v, 0, fwd_partial, bwd_partial)
         stage(
             v, LAG[4],
             lambda i: gather_third(h_of(i), sd_h.at[i], rv_h.at[i], 3),
-            lambda i: gather_third(d_all.at[i - nc], sd_dl.at[i - nc], rv_dl.at[i - nc], 2),
+            lambda i: some(i - nc, gather_third),
         )
         stage(
             v, LAG[3],
             lambda i: gather_second(h_of(i), sd_h.at[i], rv_h.at[i], 3),
-            lambda i: gather_second(d_all.at[i - nc], sd_dl.at[i - nc], rv_dl.at[i - nc], 2),
+            lambda i: some(i - nc, gather_second),
         )
         stage(v, LAG[2], fwd_sum, bwd_sum)
+        stage(v, 0, fwd_partial, bwd_partial)
         stage(v, LAG[2] + 1, lambda i: sum_sent(i, 2 * CW), lambda i: sum_sent(i, CW))
         stage(v, LAG[1], lambda i: sum_third(i, 2 * CW), lambda i: sum_third(i, CW))
         stage(v, LAG[0], lambda i: sum_second(i, 2 * CW), lambda i: sum_second(i, CW))

time: 208 us -> 205 us (0.986)
  Pallas kernels: 207 us -> 204 us
    pallas_call x1, Pallas kernels: 198 us -> 195 us  [per_device(): pl.pallas_call(functools.partial(kernel, (nt, td, dd, tq, fh, nc)), name=...]
where the time goes in v4:
time: 205 us
  Pallas kernels  204 us (100%)
    pallas_call x1, Pallas kernels, per_device(): pl.pallas_call(functools.partial(kernel, (nt, td, dd, tq, fh, nc)), name=...  195 us
    pallas_call x1, Pallas kernels, per_device(): pl.pallas_call(hand_over, name='hand_over', out_shape=tuple((jax.ShapeDty...  8.77 us

profile of v4, /device:TPU:1, one launch (start us, length us, event | category | flops | bytes accessed | tf_op | source)
XLA Modules:
  0.0 204.6 jit_solution(14063319228791462557)
XLA Ops:
  0.6 195.2 %swiglu.1 = (bf16[128,512]{1,0:T(8,128)(2,1)}, bf16[128,512]{1,0:T(8,128)(2,1)}, bf16[512,3584]{1,0:T(8,128)(2,1)}, bf16[512,3584]{1,0:T(8,128)(2,1)}, bf16[3584,512]{1,0:T(8,128)(2,1)}) custom-call(bf16[128,512]{1,0:T(8,128)(2,1)} %tok.1, bf16[512,3584]{1,0:T(8,128)(2,1)} %wg.1, bf16[512,3584]{1,0:T(8,128)(2,1)} %wu.1, bf16[3584,512]{1,0:T(8,128)(2,1)} %wd.1, ...), custom_call_target="tpu_custom_call" | custom-call | flops 33822867456 | bytes 22020096 | tf_op jit(solution)/shard_map/swiglu/pallas_call | solution.py:516
  195.8 8.8 %hand_over.1 = (bf16[128,512]{1,0:T(8,128)(2,1)}, bf16[128,512]{1,0:T(8,128)(2,1)}, bf16[512,3584]{1,0:T(8,128)(2,1)}, bf16[512,3584]{1,0:T(8,128)(2,1)}, bf16[3584,512]{1,0:T(8,128)(2,1)}) custom-call(bf16[128,512]{1,0:T(8,128)(2,1)} %get-tuple-element.10.refs_0_, bf16[128,512]{1,0:T(8,128)(2,1)} %get-tuple-element.11.refs_1_, ...), custom_call_target="tpu_custom_call" | custom-call | tf_op jit(solution)/shard_map/hand_over/pallas_call | solution.py:574

commit v5 on v4

--- a/solution.py
+++ b/solution.py
@@ -12,6 +12,7 @@
 F32 = jnp.float32
 NZ = 4
 CW = 128
+SOON = 2
 SLOTS = 8
 LAG = (2, 4, 6, 8, 10, 11)
 LATE = (3, 2)
@@ -71,6 +72,14 @@
 
     mine, theirs = at(c, dd), at(oc, dd)
 
+    @pl.loop(0, nc)
+    def _(i):
+        cols = pl.ds(pl.multiple_of(c * fh + i * CW, CW), CW)
+        for j, w in enumerate((wg, wu)):
+            pltpu.make_async_copy(w.at[:, cols], w_gu.at[i, mine, pl.ds(j * CW, CW)], ld_w.at[i]).start()
+
+    pltpu.make_async_copy(wd.at[at(c, fh), :], w_d.at[:, mine], ld_d).start()
+
     barrier = pltpu.get_barrier_semaphore()
     for near in (up_z, down_z, over_y):
         pl.semaphore_signal(barrier, inc=1, device_id=near, device_id_type=MESH)
@@ -94,17 +103,12 @@
 
     spread(0, tok, x_all)
 
-    @pl.loop(0, nc)
-    def _(i):
-        keep_cols = pl.ds(pl.multiple_of(c * fh + i * CW, CW), CW)
-        give_cols = pl.ds(pl.multiple_of(oc * fh + i * CW, CW), CW)
+    def give_weights(i):
+        cols = pl.ds(pl.multiple_of(oc * fh + i * CW, CW), CW)
         for j, w in enumerate((wg, wu)):
-            place = w_gu.at[i, mine, pl.ds(j * CW, CW)]
-            pltpu.make_async_copy(w.at[:, keep_cols], place, ld_w.at[i]).start()
-            send(w.at[:, give_cols], place, sd_w, rv_w.at[i], other)
-
-    pltpu.make_async_copy(wd.at[at(c, fh), :], w_d.at[:, mine], ld_d).start()
-    send(wd.at[at(oc, fh), :], w_d.at[:, mine], sd_d, rv_d, other)
+            send(w.at[:, cols], w_gu.at[i, mine, pl.ds(j * CW, CW)], sd_w, rv_w.at[i], other)
+
+    pl.loop(0, SOON)(give_weights)
 
     def forward_blocks(k, ref):
         order = [(1, 0), (2, 1), (4, 1), (6, 1), (2, 0), (4, 0), (6, 0), (1, 1)]
@@ -129,6 +133,8 @@
 
     forward_blocks(0, x_all)
     spread(1, og, o_all)
+    pl.loop(SOON, nc)(give_weights)
+    send(wd.at[at(oc, fh), :], w_d.at[:, mine], sd_d, rv_d, other)
     await_blocks(0, x_all)
 
     half = tokens // 2

time: 205 us -> 204 us (level)
  no operation moved by 1% of the time
where the time goes in v5:
time: 204 us
  Pallas kernels  204 us (100%)
    pallas_call x1, Pallas kernels, per_device(): pl.pallas_call(functools.partial(kernel, (nt, td, dd, tq, fh, nc)), name=...  195 us
    pallas_call x1, Pallas kernels, per_device(): pl.pallas_call(hand_over, name='hand_over', out_shape=tuple((jax.ShapeDty...  8.77 us

profile of v5, /device:TPU:1, one launch (start us, length us, event | category | flops | bytes accessed | tf_op | source)
XLA Modules:
  0.0 204.4 jit_solution(6793478258986265937)
XLA Ops:
  0.6 195.0 %swiglu.1 = (bf16[128,512]{1,0:T(8,128)(2,1)}, bf16[128,512]{1,0:T(8,128)(2,1)}, bf16[512,3584]{1,0:T(8,128)(2,1)}, bf16[512,3584]{1,0:T(8,128)(2,1)}, bf16[3584,512]{1,0:T(8,128)(2,1)}) custom-call(bf16[128,512]{1,0:T(8,128)(2,1)} %tok.1, bf16[512,3584]{1,0:T(8,128)(2,1)} %wg.1, bf16[512,3584]{1,0:T(8,128)(2,1)} %wu.1, bf16[3584,512]{1,0:T(8,128)(2,1)} %wd.1, ...), custom_call_target="tpu_custom_call" | custom-call | flops 33822867456 | bytes 22020096 | tf_op jit(solution)/shard_map/swiglu/pallas_call | solution.py:522
  195.6 8.8 %hand_over.1 = (bf16[128,512]{1,0:T(8,128)(2,1)}, bf16[128,512]{1,0:T(8,128)(2,1)}, bf16[512,3584]{1,0:T(8,128)(2,1)}, bf16[512,3584]{1,0:T(8,128)(2,1)}, bf16[3584,512]{1,0:T(8,128)(2,1)}) custom-call(bf16[128,512]{1,0:T(8,128)(2,1)} %get-tuple-element.10.refs_0_, bf16[128,512]{1,0:T(8,128)(2,1)} %get-tuple-element.11.refs_1_, ...), custom_call_target="tpu_custom_call" | custom-call | tf_op jit(solution)/shard_map/hand_over/pallas_call | solution.py:580
